TPU v7x, 512 devices: a whole 4x8x8 slice. The times are simulated.
512 devices in a mesh: row: 32 (over z, x), inw: 8 (over y_lo, core), outw: 2 (over y_hi).
Axes of the slice: x: 4, y: 8 (y_hi: 2, y_lo: 4; y = y_hi * 4 + y_lo), z: 8, core: 2. Of those that a mesh axis runs over, the one named last changes fastest.
Arguments:
- inputs: bfloat16 [768, 8192], P('row', ('inw', 'outw')), may hold values from -6 to 6
- out_grad: bfloat16 [768, 8192], P('row', ('inw', 'outw')), may hold values from -3 to 3
- gate_weight: bfloat16 [8192, 16384], P(('inw', 'outw'), 'row'), may hold values from -0.0625 to 0.0625
- up_weight: bfloat16 [8192, 16384], P(('inw', 'outw'), 'row'), may hold values from -0.0625 to 0.0625
- down_weight: bfloat16 [16384, 8192], P('row', ('inw', 'outw')), may hold values from -0.046875 to 0.046875
Outputs:
- grad_inputs: bfloat16 [768, 8192], P('row', ('inw', 'outw'))
- grad_gate: bfloat16 [8192, 16384], P(('inw', 'outw'), 'row')
- grad_up: bfloat16 [8192, 16384], P(('inw', 'outw'), 'row')
- grad_down: bfloat16 [16384, 8192], P('row', ('inw', 'outw'))
All inputs are finite; a program needn't handle non-finite values.
Results may differ from a plain program's by a relative error of at most 0.0049.
Values may be sent and summed in bfloat16 or wider, within the bound.
A program may use at most 64 MiB of HBM per device.

v0:
```python
import jax
import jax.numpy as jnp
from jax import lax
from jax.sharding import PartitionSpec as P


def contract_last(left, right):
    return lax.dot_general(
        left, right, (((1,), (1,)), ((), ())), preferred_element_type=jnp.float32
    )


def contract_first(left, right):
    return lax.dot_general(
        left, right, (((0,), (0,)), ((), ())), preferred_element_type=jnp.float32
    )


def swiglu_grads(gate_sum, up_sum, back_sum):
    sigmoid_gate = jax.nn.sigmoid(gate_sum)
    silu_gate = gate_sum * sigmoid_gate
    hidden = (silu_gate * up_sum).astype(jnp.bfloat16)
    gate_grad = (back_sum * up_sum * sigmoid_gate * (1.0 + gate_sum * (1.0 - sigmoid_gate))).astype(
        jnp.bfloat16
    )
    up_grad = (back_sum * silu_gate).astype(jnp.bfloat16)
    return (hidden, gate_grad, up_grad)


def per_device(inputs, out_grad, gate_weight, up_weight, down_weight):
    input_rows, grad_rows = (
        lax.all_gather(inputs, "row", axis=0, tiled=True),
        lax.all_gather(out_grad, "row", axis=0, tiled=True),
    )
    gate_part = jnp.dot(input_rows, gate_weight, preferred_element_type=jnp.float32)
    up_part = jnp.dot(input_rows, up_weight, preferred_element_type=jnp.float32)
    back_part = contract_last(grad_rows, down_weight)
    gate_sum, up_sum, back_sum = lax.psum((gate_part, up_part, back_part), ("inw", "outw"))
    hidden, gate_grad, up_grad = swiglu_grads(gate_sum, up_sum, back_sum)
    grad_down = contract_first(hidden, grad_rows).astype(jnp.bfloat16)
    grad_gate = contract_first(input_rows, gate_grad).astype(jnp.bfloat16)
    grad_up = contract_first(input_rows, up_grad).astype(jnp.bfloat16)
    grad_inputs = lax.psum_scatter(
        contract_last(gate_grad, gate_weight) + contract_last(up_grad, up_weight),
        "row",
        scatter_dimension=0,
        tiled=True,
    ).astype(jnp.bfloat16)
    return (grad_inputs, grad_gate, grad_up, grad_down)


def solution(mesh):
    in_specs = (
        P("row", ("inw", "outw")),
        P("row", ("inw", "outw")),
        P(("inw", "outw"), "row"),
        P(("inw", "outw"), "row"),
        P("row", ("inw", "outw")),
    )
    out_specs = (
        P("row", ("inw", "outw")),
        P(("inw", "outw"), "row"),
        P(("inw", "outw"), "row"),
        P("row", ("inw", "outw")),
    )
    return jax.shard_map(
        per_device, mesh=mesh, in_specs=in_specs, out_specs=out_specs, check_vma=False
    )
```

profile of v0, /device:TPU:8, one launch (start us, length us, event | category | flops | bytes accessed | tf_op | source)
XLA Modules:
  0.0 479.3 jit_solution(17125121648859528537)
XLA Ops:
  7.2 0.0 copy-start
  7.2 0.0 all-reduce.3.cloned.1.call-start
  7.2 56.1 %all_gather.7 = bf16[768,512]{1,0:T(8,128)(2,1)S(1)} all-gather(bf16[24,512]{1,0:T(8,128)(2,1)} %param.5), channel_id=1, replica_groups=mesh['row'=32,'inw'=8,'outw'=2] {'row'}, dimensions={0}, use_global_device_ids=true | all-gather | bytes 811008 | tf_op jit(solution)/shard_map/all_gather | solution.py:32
  63.3 48.7 %all_gather.6 = bf16[768,512]{1,0:T(8,128)(2,1)S(1)} all-gather(bf16[24,512]{1,0:T(8,128)(2,1)} %param.6), channel_id=1, replica_groups=mesh['row'=32,'inw'=8,'outw'=2] {'row'}, dimensions={0}, use_global_device_ids=true | all-gather | bytes 811008 | tf_op jit(solution)/shard_map/all_gather | solution.py:33
  112.0 0.0 copy-done
  112.0 0.0 copy-start.2
  112.0 1.7 fusion.7
  113.8 0.0 copy-done.2
  113.8 0.0 copy-start.3
  113.8 1.8 fusion.6
  115.6 0.0 copy-done.3
  115.6 1.7 fusion.5
  117.3 0.0 all-reduce.3.cloned.1.call-update
  117.4 0.0 reduce-scatter.2.cloned.1.call-start
  117.4 122.6 %all-reduce.3.cloned.1.call-done = (f32[768,512]{1,0:T(8,128)}, f32[768,512]{1,0:T(8,128)}, f32[768,512]{1,0:T(8,128)}) async-done(((f32[768,512]{1,0:T(8,128)}, f32[768,512]{1,0:T(8,128)}, f32[768,512]{1,0:T(8,128)}), (f32[768,512]{1,0:T(8,128)}, f32[768,512]{1,0:T(8,128)}, f32[768,512]{1,0:T(8,128)})) %all-reduce.3.cloned.1.call-update) | async-done | bytes 4718608 | tf_op jit(solution)/shard_map/psum | solution.py:38
  240.0 3.2 multiply_convert_fusion.1
  243.3 0.0 copy-start.1
  243.3 0.6 fusion.8
  243.9 0.3 copy-done.1
  244.2 1.8 convolution_add_fusion
  246.0 0.0 reduce-scatter.2.cloned.1.call-update
  246.0 0.6 fusion.1
  246.6 1.0 copy.9
  247.6 1.7 fusion.2
  249.3 1.0 copy.10
  250.3 3.3 convolution_convert_fusion
  253.7 217.4 %reduce-scatter.2.cloned.1.call-done = f32[24,512]{1,0:T(8,128)} async-done(((f32[768,512]{1,0:T(8,128)}), f32[24,512]{1,0:T(8,128)}) %reduce-scatter.2.cloned.1.call-update) | async-done | bytes 49168 | tf_op jit(solution)/shard_map/reduce_scatter | solution.py:43
  471.0 1.4 convert_element_type.29
Async XLA Ops:
  7.2 104.9 %copy-start = (bf16[512,512]{1,0:T(8,128)(2,1)S(1)}, bf16[512,512]{1,0:T(8,128)(2,1)}, u32[]{:S(2)}) copy-start(bf16[512,512]{1,0:T(8,128)(2,1)} %param.7) | copy-start | bytes 1572868
  7.2 232.9 %all-reduce.3.cloned.1.call-start = ((), (), s32[]{:S(2)}) async-start(), calls=%async_computation.2 | async-start | bytes 9437184 | tf_op jit(solution)/shard_map/psum | solution.py:38
  112.0 1.7 copy-start.2
  113.8 1.8 copy-start.3
  117.4 353.7 %reduce-scatter.2.cloned.1.call-start = ((), (), s32[]{:S(2)}) async-start(), calls=%async_computation.1 | async-start | bytes 1622016 | tf_op jit(solution)/shard_map/reduce_scatter | solution.py:43
  243.3 0.9 copy-start.1
Sparse Core Ops, SparseCore 0:
  117.5 122.5 all-reduce.2
  246.1 224.8 reduce-scatter.1
where the time goes:
time: 480 us; the launch traced here: 479 us
  waiting for transfers between devices  340 us (71%)
  blocking collectives  105 us (22%)
  between operations  14.1 us (3%)
  matrix products  13.3 us (3%)
    reduce_scatter x1, waiting for transfers between devices, per_device(): lax.psum_scatter(contract_last(gate_grad, gate_weight) + contract_last(up...  217 us
    psum x1, waiting for transfers between devices, per_device(): lax.psum((gate_part, up_part, back_part), ('inw', 'outw'))  123 us
    all_gather x1, blocking collectives, per_device(): lax.all_gather(inputs, 'row', axis=0, tiled=True)  56.1 us
    all_gather x1, blocking collectives, per_device(): lax.all_gather(out_grad, 'row', axis=0, tiled=True)  48.7 us
  transfers between devices with their start and end apart: 2, of which 2 were waited for; matrix products, arithmetic and copies ran while one was open for 2% of the time, Pallas kernels for 0%

commit v1 on v0

--- a/solution.py
+++ b/solution.py
@@ -35,7 +35,7 @@
     gate_part = jnp.dot(input_rows, gate_weight, preferred_element_type=jnp.float32)
     up_part = jnp.dot(input_rows, up_weight, preferred_element_type=jnp.float32)
     back_part = contract_last(grad_rows, down_weight)
-    gate_sum, up_sum, back_sum = lax.psum((gate_part, up_part, back_part), ("inw", "outw"))
+    gate_sum, up_sum, back_sum = lax.psum(lax.psum((gate_part, up_part, back_part), "outw"), "inw")
     hidden, gate_grad, up_grad = swiglu_grads(gate_sum, up_sum, back_sum)
     grad_down = contract_first(hidden, grad_rows).astype(jnp.bfloat16)
     grad_gate = contract_first(input_rows, gate_grad).astype(jnp.bfloat16)

time: 480 us -> 719 us (1.50)
  waiting for transfers between devices: 340 us -> 579 us
    psum x1 -> x2, waiting for transfers between devices: 123 us -> 362 us  [the longest x1 239 us: per_device(): lax.psum((gate_part, up_part, back_part), 'outw')]
  transfers between devices with their start and end apart: 2 -> 3, of which waited for: 2 -> 3; matrix products, arithmetic and copies ran while one was open for 2% -> 1% of each run, Pallas kernels for 0% -> 0%
where the time goes in v1:
time: 719 us; the launch traced here: 718 us
  waiting for transfers between devices  579 us (81%)
  blocking collectives  105 us (15%)
  between operations  13.8 us (2%)
  matrix products  13.3 us (2%)
    psum x1, waiting for transfers between devices, per_device(): lax.psum((gate_part, up_part, back_part), 'outw')  239 us
    reduce_scatter x1, waiting for transfers between devices, per_device(): lax.psum_scatter(contract_last(gate_grad, gate_weight) + contract_last(up...  217 us
    psum x1, waiting for transfers between devices, per_device(): lax.psum(lax.psum((gate_part, up_part, back_part), 'outw'), 'inw')  123 us
    all_gather x1, blocking collectives, per_device(): lax.all_gather(inputs, 'row', axis=0, tiled=True)  56.1 us
    all_gather x1, blocking collectives, per_device(): lax.all_gather(out_grad, 'row', axis=0, tiled=True)  48.7 us
  transfers between devices with their start and end apart: 3, of which 3 were waited for; matrix products, arithmetic and copies ran while one was open for 1% of the time, Pallas kernels for 0%

profile of v1, /device:TPU:8, one launch (start us, length us, event | category | flops | bytes accessed | tf_op | source)
XLA Modules:
  0.0 718.2 jit_solution(13808978165311741893)
XLA Ops:
  7.2 0.0 copy-start
  7.2 0.0 all-reduce.7.cloned.1.call-start
  7.2 56.1 %all_gather.7 = bf16[768,512]{1,0:T(8,128)(2,1)S(1)} all-gather(bf16[24,512]{1,0:T(8,128)(2,1)} %param.5), channel_id=1, replica_groups=mesh['row'=32,'inw'=8,'outw'=2] {'row'}, dimensions={0}, use_global_device_ids=true | all-gather | bytes 811008 | tf_op jit(solution)/shard_map/all_gather | solution.py:32
  63.3 48.7 %all_gather.6 = bf16[768,512]{1,0:T(8,128)(2,1)S(1)} all-gather(bf16[24,512]{1,0:T(8,128)(2,1)} %param.6), channel_id=1, replica_groups=mesh['row'=32,'inw'=8,'outw'=2] {'row'}, dimensions={0}, use_global_device_ids=true | all-gather | bytes 811008 | tf_op jit(solution)/shard_map/all_gather | solution.py:33
  112.0 0.0 copy-done
  112.0 0.0 copy-start.2
  112.0 1.7 fusion.7
  113.8 0.0 copy-done.2
  113.8 0.0 copy-start.3
  113.8 1.8 fusion.6
  115.6 0.0 copy-done.3
  115.6 1.8 fusion.5
  117.3 0.0 all-reduce.7.cloned.1.call-update
  117.3 0.0 all-reduce.5.cloned.1.call-start
  117.4 239.2 %all-reduce.7.cloned.1.call-done = (f32[768,512]{1,0:T(8,128)}, f32[768,512]{1,0:T(8,128)}, f32[768,512]{1,0:T(8,128)}) async-done(((f32[768,512]{1,0:T(8,128)}, f32[768,512]{1,0:T(8,128)}, f32[768,512]{1,0:T(8,128)}), (f32[768,512]{1,0:T(8,128)}, f32[768,512]{1,0:T(8,128)}, f32[768,512]{1,0:T(8,128)})) %all-reduce.7.cloned.1.call-update) | async-done | bytes 4718608 | tf_op jit(solution)/shard_map/psum | solution.py:38
  356.6 0.0 all-reduce.5.cloned.1.call-update
  356.6 0.0 reduce-scatter.2.cloned.1.call-start
  356.7 122.6 %all-reduce.5.cloned.1.call-done = (f32[768,512]{1,0:T(8,128)}, f32[768,512]{1,0:T(8,128)}, f32[768,512]{1,0:T(8,128)}) async-done(((f32[768,512]{1,0:T(8,128)}, f32[768,512]{1,0:T(8,128)}, f32[768,512]{1,0:T(8,128)}), (f32[768,512]{1,0:T(8,128)}, f32[768,512]{1,0:T(8,128)}, f32[768,512]{1,0:T(8,128)})) %all-reduce.5.cloned.1.call-update) | async-done | bytes 4718608 | tf_op jit(solution)/shard_map/psum | solution.py:38
  479.3 3.2 multiply_convert_fusion.1
  482.5 0.0 copy-start.1
  482.5 0.6 fusion.8
  483.1 0.3 copy-done.1
  483.4 1.8 convolution_add_fusion
  485.2 0.0 reduce-scatter.2.cloned.1.call-update
  485.3 0.6 fusion.1
  485.9 1.0 copy.9
  486.9 1.7 fusion.2
  488.6 1.0 copy.10
  489.6 3.3 convolution_convert_fusion
  492.9 217.4 %reduce-scatter.2.cloned.1.call-done = f32[24,512]{1,0:T(8,128)} async-done(((f32[768,512]{1,0:T(8,128)}), f32[24,512]{1,0:T(8,128)}) %reduce-scatter.2.cloned.1.call-update) | async-done | bytes 49168 | tf_op jit(solution)/shard_map/reduce_scatter | solution.py:43
  710.3 1.4 convert_element_type.29
Async XLA Ops:
  7.2 104.9 %copy-start = (bf16[512,512]{1,0:T(8,128)(2,1)S(1)}, bf16[512,512]{1,0:T(8,128)(2,1)}, u32[]{:S(2)}) copy-start(bf16[512,512]{1,0:T(8,128)(2,1)} %param.7) | copy-start | bytes 1572868
  7.2 349.4 %all-reduce.7.cloned.1.call-start = ((), (), s32[]{:S(2)}) async-start(), calls=%async_computation.3 | async-start | bytes 9437184 | tf_op jit(solution)/shard_map/psum | solution.py:38
  112.0 1.7 copy-start.2
  113.8 1.8 copy-start.3
  117.3 361.9 %all-reduce.5.cloned.1.call-start = ((), (), s32[]{:S(2)}) async-start(), calls=%async_computation.2 | async-start | bytes 9437184 | tf_op jit(solution)/shard_map/psum | solution.py:38
  356.6 353.7 %reduce-scatter.2.cloned.1.call-start = ((), (), s32[]{:S(2)}) async-start(), calls=%async_computation.1 | async-start | bytes 1622016 | tf_op jit(solution)/shard_map/reduce_scatter | solution.py:43
  482.5 0.9 copy-start.1
Sparse Core Ops, SparseCore 0:
  117.5 239.1 all-reduce.6
  360.1 119.1 all-reduce.4
  485.4 224.8 reduce-scatter.1
